TPU v7x, 128 devices: a whole 4x4x4 slice. The times are simulated.
128 devices in a mesh: dp: 32 (over z, x, core), pool: 4 (over y).
Axes of the slice: x: 4, y: 4, z: 4, core: 2. Of those that a mesh axis runs over, the one named last changes fastest.
Arguments:
- queries: float32 [1024, 4096], P(('dp', 'pool')), may hold values from -1 to 1, as said below
- documents: float32 [1024, 4096], P(('dp', 'pool')), may hold values from -1 to 1
- document_pool: float32 [65536, 4096], P(('dp', 'pool')), may hold values from -1 to 1
- hard_negatives: int32 [1024, 16], P(('dp', 'pool')), may hold values from 0 to 65535, as said below
Outputs:
- averaged_objective: float32 [], replicated
- query_grad: float32 [1024, 4096], P(('dp', 'pool'))
- document_grad: float32 [1024, 4096], P(('dp', 'pool'))
- pool_grad: float32 [65536, 4096], P(('dp', 'pool'))
Inputs may be any that keep to these rules, and one draw needn't show every extreme that they name: `queries`: rows are noisy embeddings of several scales; entries lie in the stated range. `hard_negatives`: of the 128 ids held by one device, at most 2 lie in the rows k * 512 to (k + 1) * 512 - 1 for any k, and exactly 2 do so for at least 16 values of k; some ids repeat.
All inputs are finite; a program needn't handle non-finite values.
Results may differ from a plain program's by a relative error of at most 0.0003.
Values sent between devices are 32-bit elements; how exact they have to be, the bound alone decides.
No kernel may reach another device: no remote copies, remote signals or barrier semaphores. Data moves between devices by JAX's collectives and lax.ppermute only.
A program may use at most 128 MiB of HBM per device.

v0:
```python
import functools

import jax
import jax.numpy as jnp
from jax import lax
from jax.experimental import pallas as pl
from jax.experimental.pallas import tpu as pltpu
from jax.sharding import PartitionSpec as P

heat = 20.0
epsilon = 1e-06
highest = lax.Precision.HIGHEST
lanes = 128
everyone = ("dp", "pool")
capacity = 2
limit = 56 * 1024 * 1024


def halves(values):
    high = values.astype(jnp.bfloat16)
    return high, (values - high.astype(jnp.float32)).astype(jnp.bfloat16)


def dot3(left, right, contract):
    one = lambda a, b: lax.dot_general(
        a, b, (contract, ((), ())), preferred_element_type=jnp.float32
    )
    return one(left[0], right[0]) + (one(left[0], right[1]) + one(left[1], right[0]))


def pick_kernel(step_rows, wanted, pool, unit, factor, packed, held, arrived):
    step = pl.program_id(0)
    width = pool.shape[1]
    strips = width // lanes
    total = held.shape[0]

    @pl.when(step == 0)
    def _():
        def fetch(j, carry):
            pltpu.make_async_copy(
                pool.at[pl.ds(wanted[j], 1)], held.at[pl.ds(j, 1)], arrived.at[j // step_rows]
            ).start()
            return carry

        lax.fori_loop(0, total, fetch, 0, unroll=8)

    start = pl.multiple_of(step * step_rows, step_rows)
    pltpu.make_async_copy(
        pool.at[pl.ds(0, step_rows)], held.at[pl.ds(start, step_rows)], arrived.at[step]
    ).wait()
    for tile in range(step_rows // 8):
        rows = held[pl.ds(start + tile * 8, 8), :]
        scale = lax.rsqrt(jnp.sum(rows * rows, axis=1, keepdims=True) + epsilon)
        rows = rows * scale
        unit[pl.ds(tile * 8, 8), :] = rows
        factor[pl.ds(tile * 8, 8), :] = jnp.broadcast_to(scale, (8, lanes))
        for strip in range(strips):
            packed[pl.ds(tile * 8 * strips + strip, 8, stride=strips), :] = rows[
                :, strip * lanes : (strip + 1) * lanes
            ]


def pick(wanted, pool):
    total = wanted.shape[0]
    width = pool.shape[1]
    strips = width // lanes
    step_rows = 32
    return pl.pallas_call(
        functools.partial(pick_kernel, step_rows),
        grid_spec=pltpu.PrefetchScalarGridSpec(
            num_scalar_prefetch=1,
            grid=(total // step_rows,),
            in_specs=[pl.BlockSpec(memory_space=pl.ANY)],
            out_specs=[
                pl.BlockSpec((step_rows, width), lambda i, *_: (i, 0)),
                pl.BlockSpec((step_rows, lanes), lambda i, *_: (i, 0)),
                pl.BlockSpec((step_rows * strips, lanes), lambda i, *_: (i, 0)),
            ],
            scratch_shapes=[
                pltpu.VMEM((total, width), jnp.float32),
                pltpu.SemaphoreType.DMA((total // step_rows,)),
            ],
        ),
        out_shape=[
            jax.ShapeDtypeStruct((total, width), jnp.float32),
            jax.ShapeDtypeStruct((total, lanes), jnp.float32),
            jax.ShapeDtypeStruct((total * strips, lanes), jnp.float32),
        ],
        compiler_params=pltpu.CompilerParams(vmem_limit_bytes=limit),
        cost_estimate=pl.CostEstimate(flops=4 * total * width, bytes_accessed=12 * total * width, transcendentals=0),
    )(wanted, pool)


def against_kernel(packed, unit, asker, parts, mixed, rows):
    strips = rows.shape[1] // lanes
    count = rows.shape[0]
    for strip in range(strips):
        rows[:, strip * lanes : (strip + 1) * lanes] = packed[pl.ds(strip, count, stride=strips), :]
    split = halves(rows[...])
    scores = heat * dot3(halves(unit[...]), split, ((1,), (1,)))
    number = lax.broadcasted_iota(jnp.int32, scores.shape, 0)
    chosen = jnp.where(asker[...] == number, jnp.exp(scores - heat), 0.0)
    parts[...] = chosen
    mixed[...] = dot3(halves(chosen), split, ((1,), (0,)))


def against(packed, unit, asker):
    own, width = unit.shape
    count = packed.shape[0] // (width // lanes)
    return pl.pallas_call(
        against_kernel,
        out_shape=[
            jax.ShapeDtypeStruct((own, count), jnp.float32),
            jax.ShapeDtypeStruct((own, width), jnp.float32),
        ],
        scratch_shapes=[pltpu.VMEM((count, width), jnp.float32)],
        compiler_params=pltpu.CompilerParams(vmem_limit_bytes=limit),
        cost_estimate=pl.CostEstimate(flops=12 * own * count * width, bytes_accessed=4 * count * width, transcendentals=0),
    )(packed, unit, asker)


def finish_kernel(
    target, weight, queries, unit, factor, doc_unit, doc_factor,
    doc_grad, pool_grad, upstream, high, low, blank, fill_sem, row_sem,
):
    step = pl.program_id(0)
    block = queries.shape[1]
    slots = unit.shape[0]
    own = doc_unit.shape[0]
    blank_rows = blank.shape[0]
    fills = [
        pltpu.make_async_copy(blank, pool_grad.at[pl.ds(i * blank_rows, blank_rows)], fill_sem.at[i])
        for i in range(pool_grad.shape[0] // blank_rows)
    ]

    @pl.when(step == 0)
    def _():
        blank[...] = jnp.zeros_like(blank)
        for fill in fills:
            fill.start()
        first, second = halves(weight[...])
        high[...] = first
        low[...] = second

    right = halves(queries[...])
    column = pl.multiple_of(step * block, block)
    upstream[:, pl.ds(column, block)] = dot3((high[...], low[...]), right, ((1,), (0,)))

    @pl.when(step == pl.num_programs(0) - 1)
    def _():
        for fill in fills:
            fill.wait()
        above = upstream[pl.ds(slots, own), :]
        inner = jnp.sum(doc_unit[...] * above, axis=1, keepdims=True)
        doc_grad[...] = doc_factor[:, :1] * (above - doc_unit[...] * inner)

        def row_copy(j):
            return pltpu.make_async_copy(
                upstream.at[pl.ds(j, 1)], pool_grad.at[pl.ds(target[j], 1)], row_sem
            )

        def settle(tile, carry):
            rows = pl.ds(pl.multiple_of(tile * 8, 8), 8)
            above = upstream[rows, :]
            unit_rows = unit[rows, :]
            inner = jnp.sum(unit_rows * above, axis=1, keepdims=True)
            upstream[rows, :] = factor[rows, :1] * (above - unit_rows * inner)
            for i in range(8):
                @pl.when(target[tile * 8 + i] >= 0)
                def _():
                    row_copy(tile * 8 + i).start()
            return carry

        lax.fori_loop(0, slots // 8, settle, 0)

        def drain(j, carry):
            @pl.when(target[j] >= 0)
            def _():
                row_copy(j).wait()
            return carry

        lax.fori_loop(0, slots, drain, 0)


def finish(target, weight, queries, unit, factor, doc_unit, doc_factor, pool_rows):
    slots, width = unit.shape
    own = doc_unit.shape[0]
    batch = queries.shape[0]
    block = 512
    whole = lambda a: pl.BlockSpec(a.shape, lambda i, *_: (0, 0))
    blank_rows = 64
    return pl.pallas_call(
        finish_kernel,
        grid_spec=pltpu.PrefetchScalarGridSpec(
            num_scalar_prefetch=1,
            grid=(width // block,),
            in_specs=[
                whole(weight),
                pl.BlockSpec((batch, block), lambda i, *_: (0, i)),
                whole(unit),
                whole(factor),
                whole(doc_unit),
                whole(doc_factor),
            ],
            out_specs=[whole(doc_unit), pl.BlockSpec(memory_space=pl.ANY)],
            scratch_shapes=[
                pltpu.VMEM((slots + own, width), jnp.float32),
                pltpu.VMEM((slots + own, batch), jnp.bfloat16),
                pltpu.VMEM((slots + own, batch), jnp.bfloat16),
                pltpu.VMEM((blank_rows, width), jnp.float32),
                pltpu.SemaphoreType.DMA((pool_rows // blank_rows,)),
                pltpu.SemaphoreType.DMA,
            ],
        ),
        out_shape=[
            jax.ShapeDtypeStruct((own, width), jnp.float32),
            jax.ShapeDtypeStruct((pool_rows, width), jnp.float32),
        ],
        compiler_params=pltpu.CompilerParams(vmem_limit_bytes=limit),
        cost_estimate=pl.CostEstimate(
            flops=6 * (slots + own) * batch * width, bytes_accessed=4 * width * (batch + pool_rows + slots), transcendentals=0
        ),
    )(target, weight, queries, unit, factor, doc_unit, doc_factor)


def factor_of(values):
    return lax.rsqrt(jnp.sum(values * values, axis=-1, keepdims=True) + epsilon)


def dot(left, right, contract):
    return lax.dot_general(
        left, right, (contract, ((), ())), precision=highest, preferred_element_type=jnp.float32
    )


def back(factor, unit, upstream):
    return factor * (upstream - unit * jnp.sum(unit * upstream, axis=-1, keepdims=True))


def local(queries, documents, document_pool, hard_negatives):
    own, width = queries.shape
    strips = width // lanes
    pool_rows = document_pool.shape[0]
    neg = hard_negatives.shape[1]
    pool_size = lax.axis_size("pool")
    groups = lax.axis_size("dp")
    devices = groups * pool_size
    batch = own * devices
    slots = devices * capacity
    ids = own * neg
    member = lax.axis_index("pool")
    me = lax.axis_index("dp") * pool_size + member

    def forward(values, steps):
        return lax.ppermute(
            values, "pool", [(i, (i + steps) % pool_size) for i in range(pool_size)]
        )

    def exchange(values):
        return lax.all_to_all(values, everyone, split_axis=0, concat_axis=0, tiled=True)

    flat = hard_negatives.reshape(-1)
    owner = flat // pool_rows
    order = jnp.arange(ids, dtype=jnp.int32)
    earlier = (owner[:, None] == owner[None, :]) & (order[None, :] < order[:, None])
    slot = owner * capacity + jnp.sum(earlier.astype(jnp.int32), axis=1)
    asker = order // neg
    code = (flat - owner * pool_rows) * own + asker
    taken = slot[None, :] == jnp.arange(slots, dtype=jnp.int32)[:, None]
    request = jnp.sum(jnp.where(taken, code[None, :] + 1, 0), axis=1) - 1
    slot_query = jnp.sum(jnp.where(taken, asker[None, :] + 1, 0), axis=1) - 1
    arrived = exchange(request.reshape(devices, capacity)).reshape(-1)

    query_factor = factor_of(queries)
    doc_factor = factor_of(documents)
    doc_unit = documents * doc_factor
    query_unit, arrived = lax.optimization_barrier((queries * query_factor, arrived))

    valid = arrived >= 0
    wanted = jnp.maximum(arrived, 0)
    named_row = wanted // own
    source = jnp.arange(slots, dtype=jnp.int32) // capacity
    place = (
        source // pool_size * pool_size + (source - member) % pool_size
    ) * own + wanted % own
    row_unit, row_factor, packed = pick(named_row, document_pool)
    neg_rows = exchange(packed.reshape(devices, capacity * strips, lanes))

    cohort = jnp.concatenate(
        [query_unit] + [forward(query_unit, -steps) for steps in range(1, pool_size)], axis=0
    )
    passages = lax.all_gather(doc_unit, "dp", axis=0, tiled=True)
    everything = lax.all_gather(cohort, "dp", axis=0, tiled=True)

    parts = jnp.exp(heat * dot(cohort, passages, ((1,), (1,))) - heat)
    sums = jnp.sum(parts, axis=1, keepdims=True)
    mixed = dot(parts, passages, ((1,), (0,)))
    payload = jnp.concatenate([mixed, jnp.broadcast_to(sums, (sums.shape[0], lanes))], axis=1)
    shares = payload[:own]
    for steps in range(1, pool_size):
        shares = shares + forward(payload[steps * own : (steps + 1) * own], steps)

    neg_parts, neg_mixed = against(
        neg_rows.reshape(slots * strips, lanes), query_unit, slot_query[None, :]
    )
    totals = shares[:, width] + jnp.sum(neg_parts, axis=1)
    upstream = heat * ((shares[:, :width] + neg_mixed) / totals[:, None] - doc_unit)
    query_grad = back(query_factor, query_unit, upstream)

    diagonal = heat * jnp.sum(query_unit * doc_unit, axis=1)
    slot_weight = heat * jnp.sum(neg_parts / totals[:, None], axis=0)
    block = parts.reshape(own * pool_size, groups, own).transpose(1, 2, 0).reshape(groups, 1, -1)
    here = jnp.arange(pool_size, dtype=jnp.int32)[None, :, None] == member
    news = jnp.concatenate(
        [
            jnp.where(here, block, 0.0).reshape(devices, -1),
            jnp.broadcast_to(totals, (devices, own)),
            jnp.broadcast_to(diagonal, (devices, own)),
            slot_weight.reshape(devices, capacity),
        ],
        axis=1,
    )
    news = exchange(news)
    edge = own * own * pool_size
    doc_parts = jnp.sum(news[:, :edge].reshape(groups, pool_size, edge), axis=1)
    doc_parts = doc_parts.reshape(groups, own, own * pool_size).transpose(1, 0, 2)
    all_totals = news[:, edge : edge + own]
    all_diagonal = news[:, edge + own : edge + 2 * own]
    slot_weight = news[:, edge + 2 * own :].reshape(-1)
    objective = jnp.sum(jnp.log(all_totals) + heat - all_diagonal) / batch
    placed_totals = jnp.roll(
        all_totals.reshape(groups, pool_size, own), -member, axis=1
    ).reshape(batch)

    number = jnp.arange(batch, dtype=jnp.int32)
    row = jnp.arange(own, dtype=jnp.int32)[:, None]
    matched = number[None, :] == me // pool_size * pool_size * own + row
    doc_weight = heat * (
        doc_parts.reshape(own, batch) / placed_totals[None, :] - matched.astype(jnp.float32)
    )
    spread = jnp.where(place[:, None] == number[None, :], slot_weight[:, None], 0.0)
    same = (named_row[:, None] == named_row[None, :]) & valid[None, :]
    spread = dot(same.astype(jnp.float32), spread, ((1,), (0,)))
    slot_order = jnp.arange(slots, dtype=jnp.int32)
    repeated = jnp.any(same & (slot_order[None, :] < slot_order[:, None]), axis=1)
    target = jnp.where(valid & ~repeated, named_row, -1)
    document_grad, pool_grad = finish(
        target,
        jnp.concatenate([spread, doc_weight], axis=0),
        everything,
        row_unit,
        row_factor,
        doc_unit,
        jnp.broadcast_to(doc_factor, (own, lanes)),
        pool_rows,
    )
    return (objective, query_grad, document_grad, pool_grad)


def solution(mesh):
    rows = P(everyone, None)
    return jax.shard_map(
        local,
        mesh=mesh,
        in_specs=(rows, rows, rows, rows),
        out_specs=(P(), rows, rows, rows),
        check_vma=False,
    )
```

profile of v0, /device:TPU:1, one launch (start us, length us, event | category | flops | bytes accessed | tf_op | source)
XLA Modules:
  0.0 211.8 jit_solution(17309626681669728052)
XLA Ops:
  7.2 1.1 multiply_reduce_fusion.2
  8.3 1.6 broadcast_multiply_fusion.doc_unit
  11.8 11.5 %all-to-all-start = ((s32[128,1,2]{2,1,0:T(1,128)}), s32[128,1,2]{2,1,0:T(1,128)S(1)}, u32[]{:S(2)}, u32[]{:S(2)}) async-start(s32[128,1,2]{2,1,0:T(1,128)} %bitcast), calls=%async_computation | async-start | bytes 131072 | tf_op jit(solution)/shard_map/all_to_all | solution.py:260
  23.4 1.1 multiply_reduce_fusion.3
  24.5 1.0 broadcast_multiply_fusion.1.unit
  25.5 7.5 %all-to-all-done = s32[128,1,2]{2,1,0:T(1,128)S(1)} async-done(((s32[128,1,2]{2,1,0:T(1,128)}), s32[128,1,2]{2,1,0:T(1,128)S(1)}, u32[]{:S(2)}, u32[]{:S(2)}) %all-to-all-start) | async-done | bytes 1056 | tf_op jit(solution)/shard_map/all_to_all | solution.py:260
  34.8 1.9 collective-permute-start.1
  37.5 5.2 %collective-permute-done = f32[8,4096]{1,0:T(8,128)S(1)} collective-permute-done((f32[8,4096]{1,0:T(8,128)S(1)}, f32[8,4096]{1,0:T(8,128)S(1)}, u32[]{:S(2)}, u32[]{:S(2)}) %collective-permute-start) | collective-permute-done | bytes 131104 | tf_op jit(solution)/shard_map/ppermute | solution.py:255
  42.8 0.8 copy-done.2
  44.2 13.3 %shard_map.75 = (f32[256,4096]{1,0:T(8,128)}, f32[256,128]{1,0:T(8,128)}, f32[8192,128]{1,0:T(8,128)}) custom-call(s32[256]{0:T(256)} %get-tuple-element.37.wanted, f32[512,4096]{1,0:T(8,128)} %pool.1), custom_call_target="tpu_custom_call" | custom-call | flops 4194304 | bytes 12582912 | tf_op jit(solution)/shard_map/pallas_call | solution.py:68
  57.5 8.5 %all-to-all-start.1 = ((f32[128,64,128]{2,1,0:T(8,128)}), f32[128,64,128]{2,1,0:T(8,128)}, u32[]{:S(2)}, u32[]{:S(2)}) async-start(f32[128,64,128]{2,1,0:T(8,128)} %bitcast.17), calls=%async_computation.1 | async-start | bytes 8388608 | tf_op jit(solution)/shard_map/all_to_all | solution.py:260
  67.6 59.7 %all-to-all-done.1 = f32[128,64,128]{2,1,0:T(8,128)} async-done(((f32[128,64,128]{2,1,0:T(8,128)}), f32[128,64,128]{2,1,0:T(8,128)}, u32[]{:S(2)}, u32[]{:S(2)}) %all-to-all-start.1) | async-done | bytes 4194336 | tf_op jit(solution)/shard_map/all_to_all | solution.py:260
  127.3 8.6 %shard_map.76 = (f32[8,256]{1,0:T(8,128)}, f32[8,4096]{1,0:T(8,128)}) custom-call(f32[8192,128]{1,0:T(8,128)} %bitcast.4.packed, f32[8,4096]{1,0:T(8,128)} %copy-done, s32[1,256]{1,0:T(1,128)} %bitcast.24), custom_call_target="tpu_custom_call" | custom-call | flops 100663296 | bytes 4194304 | tf_op jit(solution)/shard_map/pallas_call | solution.py:110
  136.8 6.3 %fusion.30 = (f32[32]{0:T(128)S(1)}, f32[32,256]{1,0:T(8,128)S(1)}) fusion(f32[32,4096]{1,0:T(8,128)S(1)} %copy-done.3, f32[256,4096]{1,0:T(8,128)} %all-gather.3.cloned.1.call-done), kind=kOutput, calls=%fused_computation.103 | convolution fusion | flops 402677728 | bytes 4751488 | tf_op jit(solution)/shard_map/dot_general | solution.py:231
  143.5 4.8 %fusion.31 = f32[32,4096]{1,0:T(8,128)S(1)} fusion(f32[32,256]{1,0:T(8,128)S(1)} %get-tuple-element.39, f32[256,4096]{1,0:T(8,128)} %all-gather.3.cloned.1.call-done), kind=kOutput, calls=%fused_computation.104 | convolution fusion | flops 402653184 | bytes 4751360 | tf_op jit(solution)/shard_map/dot_general | solution.py:231
  148.7 2.5 %collective-permute-start.5 = (f32[8,4224]{1,0:T(8,128)S(1)}, f32[8,4224]{1,0:T(8,128)S(1)}, u32[]{:S(2)}, u32[]{:S(2)}) collective-permute-start(f32[8,4224]{1,0:T(8,128)S(1)} %get-tuple-element.32), channel_id=1, source_target_pairs={{0,3},{1,0},{2,1},{3,2},{4,7},{5,4},{6,5},{7,6},{8,11},{9,8},{10,9... | collective-permute-start | bytes 405512 | tf_op jit(solution)/shard_map/ppermute | solution.py:255
  151.2 4.1 %collective-permute-done.3 = f32[8,4224]{1,0:T(8,128)S(1)} collective-permute-done((f32[8,4224]{1,0:T(8,128)S(1)}, f32[8,4224]{1,0:T(8,128)S(1)}, u32[]{:S(2)}, u32[]{:S(2)}) %collective-permute-start.3) | collective-permute-done | bytes 135200 | tf_op jit(solution)/shard_map/ppermute | solution.py:255
  155.3 1.7 collective-permute-done.5
  158.6 0.9 copy.48
  159.5 5.1 %all-to-all-start.2 = ((f32[128,1,274]{2,1,0:T(1,128)}), f32[128,1,274]{2,1,0:T(1,128)S(1)}, u32[]{:S(2)}, u32[]{:S(2)}) async-start(f32[128,1,274]{2,1,0:T(1,128)} %copy.48), calls=%async_computation.2 | async-start | bytes 393216 | tf_op jit(solution)/shard_map/all_to_all | solution.py:260
  165.3 9.7 %all-to-all-done.2 = f32[128,1,274]{2,1,0:T(1,128)S(1)} async-done(((f32[128,1,274]{2,1,0:T(1,128)}), f32[128,1,274]{2,1,0:T(1,128)S(1)}, u32[]{:S(2)}, u32[]{:S(2)}) %all-to-all-start.2) | async-done | bytes 140320 | tf_op jit(solution)/shard_map/all_to_all | solution.py:260
  177.6 0.9 fusion.2
  178.5 1.1 pad_maximum_fusion.weight
  180.3 23.5 %shard_map.77 = (f32[8,4096]{1,0:T(8,128)}, f32[512,4096]{1,0:T(8,128)}) custom-call(s32[256]{0:T(256)} %and_select_fusion.4.target, f32[264,1024]{1,0:T(8,128)} %pad_maximum_fusion.weight, f32[1024,4096]{1,0:T(8,128)} %all-gather.5.cloned.1.call-done.queries, f32[256,4096]{1,0:T(8,128)} %get-tuple-element.18.unit, f32[256,128]{1,0:T(8,128)} %get-tuple-element.19.factor, ...), custom_call_target="tpu_custom_call" | custom-call | flops 6643777536 | bytes 29360128 | tf_op jit(solution)/shard_map/pallas_call | solution.py:192
  (93 shorter events, 13.2 us)
Async XLA Ops:
  7.2 129.7 %all-gather.3.cloned.1.call-start = ((), (), s32[]{:S(2)}) async-start(), calls=%async_computation.3 | async-start | bytes 4325376 | tf_op jit(solution)/shard_map/all_gather | solution.py:292
  11.8 21.1 %all-to-all-start = ((s32[128,1,2]{2,1,0:T(1,128)}), s32[128,1,2]{2,1,0:T(1,128)S(1)}, u32[]{:S(2)}, u32[]{:S(2)}) async-start(s32[128,1,2]{2,1,0:T(1,128)} %bitcast), calls=%async_computation | async-start | bytes 131072 | tf_op jit(solution)/shard_map/all_to_all | solution.py:260
  23.4 156.3 %all-gather.5.cloned.1.call-start = ((), (), s32[]{:S(2)}) async-start(), calls=%async_computation.4 | async-start | bytes 17301504 | tf_op jit(solution)/shard_map/all_gather | solution.py:293
  25.5 32.0 %copy-start = (f32[8,4096]{1,0:T(8,128)}, f32[8,4096]{1,0:T(8,128)S(1)}, u32[]{:S(2)}) copy-start(f32[8,4096]{1,0:T(8,128)S(1)} %broadcast_multiply_fusion.1.unit) | copy-start | bytes 393220
  34.4 8.3 %collective-permute-start.2 = (f32[8,4096]{1,0:T(8,128)S(1)}, f32[8,4096]{1,0:T(8,128)S(1)}, u32[]{:S(2)}, u32[]{:S(2)}) collective-permute-start(f32[8,4096]{1,0:T(8,128)S(1)} %broadcast_multiply_fusion.1.unit), channel_id=1, source_target_pairs={{0,1},{1,2},{2,3},{3,0},{4,5},{5,6},{6,7},{7,4},{8,9},{9,10},{10,1... | collective-permute-start | bytes 393224 | tf_op jit(solution)/shard_map/ppermute | solution.py:255
  34.8 7.9 %collective-permute-start.1 = (f32[8,4096]{1,0:T(8,128)S(1)}, f32[8,4096]{1,0:T(8,128)S(1)}, u32[]{:S(2)}, u32[]{:S(2)}) collective-permute-start(f32[8,4096]{1,0:T(8,128)S(1)} %broadcast_multiply_fusion.1.unit), channel_id=1, source_target_pairs={{0,2},{1,3},{2,0},{3,1},{4,6},{5,7},{6,4},{7,5},{8,10},{9,11},{10,... | collective-permute-start | bytes 393224 | tf_op jit(solution)/shard_map/ppermute | solution.py:255
  36.7 6.0 %collective-permute-start = (f32[8,4096]{1,0:T(8,128)S(1)}, f32[8,4096]{1,0:T(8,128)S(1)}, u32[]{:S(2)}, u32[]{:S(2)}) collective-permute-start(f32[8,4096]{1,0:T(8,128)S(1)} %broadcast_multiply_fusion.1.unit), channel_id=1, source_target_pairs={{0,3},{1,0},{2,1},{3,2},{4,7},{5,4},{6,5},{7,6},{8,11},{9,8},{10,9... | collective-permute-start | bytes 393224 | tf_op jit(solution)/shard_map/ppermute | solution.py:255
  42.8 0.8 copy-start.2
  57.5 9.4 %copy-start.7 = (s32[256]{0:T(256)S(1)}, s32[256]{0:T(256)}, u32[]{:S(2)}) copy-start(s32[256]{0:T(256)} %get-tuple-element.37.wanted) | copy-start | bytes 3076
  57.5 69.8 %all-to-all-start.1 = ((f32[128,64,128]{2,1,0:T(8,128)}), f32[128,64,128]{2,1,0:T(8,128)}, u32[]{:S(2)}, u32[]{:S(2)}) async-start(f32[128,64,128]{2,1,0:T(8,128)} %bitcast.17), calls=%async_computation.1 | async-start | bytes 8388608 | tf_op jit(solution)/shard_map/all_to_all | solution.py:260
  66.1 70.8 %copy-start.3 = (f32[32,4096]{1,0:T(8,128)S(1)}, f32[32,4096]{1,0:T(8,128)}, u32[]{:S(2)}) copy-start(f32[32,4096]{1,0:T(8,128)} %copy-done.2) | copy-start | bytes 1572868
  143.2 14.7 %copy-start.1 = (f32[8,4096]{1,0:T(8,128)S(1)}, f32[8,4096]{1,0:T(8,128)}, u32[]{:S(2)}) copy-start(f32[8,4096]{1,0:T(8,128)} %copy-done) | copy-start | bytes 393220
  143.2 14.7 %copy-start.4 = (f32[8,4096]{1,0:T(8,128)S(1)}, f32[8,4096]{1,0:T(8,128)}, u32[]{:S(2)}) copy-start(f32[8,4096]{1,0:T(8,128)} %param.5) | copy-start | bytes 393220
  143.2 14.7 %copy-start.5 = (f32[8,4096]{1,0:T(8,128)S(1)}, f32[8,4096]{1,0:T(8,128)}, u32[]{:S(2)}) copy-start(f32[8,4096]{1,0:T(8,128)} %get-tuple-element.17) | copy-start | bytes 393220
  143.3 15.0 %copy-start.6 = (f32[8,256]{1,0:T(8,128)S(1)}, f32[8,256]{1,0:T(8,128)}, u32[]{:S(2)}) copy-start(f32[8,256]{1,0:T(8,128)} %get-tuple-element.16) | copy-start | bytes 24580
  148.4 6.9 %collective-permute-start.3 = (f32[8,4224]{1,0:T(8,128)S(1)}, f32[8,4224]{1,0:T(8,128)S(1)}, u32[]{:S(2)}, u32[]{:S(2)}) collective-permute-start(f32[8,4224]{1,0:T(8,128)S(1)} %get-tuple-element.31), channel_id=1, source_target_pairs={{0,1},{1,2},{2,3},{3,0},{4,5},{5,6},{6,7},{7,4},{8,9},{9,10},{10,1... | collective-permute-start | bytes 405512 | tf_op jit(solution)/shard_map/ppermute | solution.py:255
  148.7 8.4 %collective-permute-start.5 = (f32[8,4224]{1,0:T(8,128)S(1)}, f32[8,4224]{1,0:T(8,128)S(1)}, u32[]{:S(2)}, u32[]{:S(2)}) collective-permute-start(f32[8,4224]{1,0:T(8,128)S(1)} %get-tuple-element.32), channel_id=1, source_target_pairs={{0,3},{1,0},{2,1},{3,2},{4,7},{5,4},{6,5},{7,6},{8,11},{9,8},{10,9... | collective-permute-start | bytes 405512 | tf_op jit(solution)/shard_map/ppermute | solution.py:255
  151.2 6.5 %collective-permute-start.4 = (f32[8,4224]{1,0:T(8,128)S(1)}, f32[8,4224]{1,0:T(8,128)S(1)}, u32[]{:S(2)}, u32[]{:S(2)}) collective-permute-start(f32[8,4224]{1,0:T(8,128)S(1)} %get-tuple-element.33), channel_id=1, source_target_pairs={{0,2},{1,3},{2,0},{3,1},{4,6},{5,7},{6,4},{7,5},{8,10},{9,11},{10,... | collective-permute-start | bytes 405512 | tf_op jit(solution)/shard_map/ppermute | solution.py:255
  159.5 15.5 %all-to-all-start.2 = ((f32[128,1,274]{2,1,0:T(1,128)}), f32[128,1,274]{2,1,0:T(1,128)S(1)}, u32[]{:S(2)}, u32[]{:S(2)}) async-start(f32[128,1,274]{2,1,0:T(1,128)} %copy.48), calls=%async_computation.2 | async-start | bytes 393216 | tf_op jit(solution)/shard_map/all_to_all | solution.py:260
Sparse Core Ops, SparseCore 0:
  10.3 50.0 all-gather.2
  62.6 107.8 all-gather.4
where the time goes:
time: 213 us; the launch traced here: 212 us
  waiting for transfers between devices  88.5 us (42%)
  Pallas kernels  45.4 us (21%)
  starting transfers between devices  31 us (15%)
  between operations  16.3 us (8%)
  other arithmetic  12 us (6%)
  matrix products  12 us (6%)
  local copies, waits for them, and re-layouts  6.51 us (3%)
    all_to_all x3, waiting for transfers between devices, exchange(): lax.all_to_all(values, everyone, split_axis=0, concat_axis=0, tiled=True)  76.8 us
    all_to_all x3, starting transfers between devices, exchange(): lax.all_to_all(values, everyone, split_axis=0, concat_axis=0, tiled=True)  25.1 us
    pallas_call x1, Pallas kernels, finish(): pl.pallas_call(finish_kernel, grid_spec=pltpu.PrefetchScalarGridSpec(num_...  23.5 us
    pallas_call x1, Pallas kernels, pick(): pl.pallas_call(functools.partial(pick_kernel, step_rows), grid_spec=pltpu...  13.3 us
    dot_general x3, matrix products, dot(): lax.dot_general(left, right, (contract, ((), ())), precision=highest, pre...  12 us
    ppermute x6, waiting for transfers between devices, forward(): lax.ppermute(values, 'pool', [(i, (i + steps) % pool_size) for i in range...  11.6 us
    pallas_call x1, Pallas kernels, against(): pl.pallas_call(against_kernel, out_shape=[jax.ShapeDtypeStruct((own, coun...  8.6 us
    ppermute x6, starting transfers between devices, forward(): lax.ppermute(values, 'pool', [(i, (i + steps) % pool_size) for i in range...  5.82 us
  transfers between devices with their start and end apart: 11, of which 7 were waited for; matrix products, arithmetic and copies ran while one was open for 12% of the time, Pallas kernels for 10%

commit v1 on v0

--- a/solution.py
+++ b/solution.py
@@ -91,9 +91,17 @@
     )(wanted, pool)
 
 
-def against_kernel(packed, unit, asker, parts, mixed, rows):
+def against_kernel(packed, unit, asker, parts, mixed, blank, rows, zeros, fill_sem):
     strips = rows.shape[1] // lanes
     count = rows.shape[0]
+    zero_rows = zeros.shape[0]
+    zeros[...] = jnp.zeros_like(zeros)
+    fills = [
+        pltpu.make_async_copy(zeros, blank.at[pl.ds(i * zero_rows, zero_rows)], fill_sem.at[i])
+        for i in range(blank.shape[0] // zero_rows)
+    ]
+    for fill in fills:
+        fill.start()
     for strip in range(strips):
         rows[:, strip * lanes : (strip + 1) * lanes] = packed[pl.ds(strip, count, stride=strips), :]
     split = halves(rows[...])
@@ -102,125 +110,139 @@
     chosen = jnp.where(asker[...] == number, jnp.exp(scores - heat), 0.0)
     parts[...] = chosen
     mixed[...] = dot3(halves(chosen), split, ((1,), (0,)))
-
-
-def against(packed, unit, asker):
+    for fill in fills:
+        fill.wait()
+
+
+def against(packed, unit, asker, pool_rows):
     own, width = unit.shape
     count = packed.shape[0] // (width // lanes)
+    zero_rows = 64
+    vmem = pl.BlockSpec(memory_space=pltpu.VMEM)
     return pl.pallas_call(
         against_kernel,
+        out_specs=[vmem, vmem, pl.BlockSpec(memory_space=pl.ANY)],
         out_shape=[
             jax.ShapeDtypeStruct((own, count), jnp.float32),
             jax.ShapeDtypeStruct((own, width), jnp.float32),
-        ],
-        scratch_shapes=[pltpu.VMEM((count, width), jnp.float32)],
+            jax.ShapeDtypeStruct((pool_rows, width), jnp.float32),
+        ],
+        scratch_shapes=[
+            pltpu.VMEM((count, width), jnp.float32),
+            pltpu.VMEM((zero_rows, width), jnp.float32),
+            pltpu.SemaphoreType.DMA((pool_rows // zero_rows,)),
+        ],
         compiler_params=pltpu.CompilerParams(vmem_limit_bytes=limit),
-        cost_estimate=pl.CostEstimate(flops=12 * own * count * width, bytes_accessed=4 * count * width, transcendentals=0),
+        cost_estimate=pl.CostEstimate(
+            flops=12 * own * count * width, bytes_accessed=4 * width * (count + pool_rows), transcendentals=0
+        ),
     )(packed, unit, asker)
 
 
 def finish_kernel(
-    target, weight, queries, unit, factor, doc_unit, doc_factor,
-    doc_grad, pool_grad, upstream, high, low, blank, fill_sem, row_sem,
+    block, count, slot_of, row_of, weight, queries, unit, factor, doc_unit, doc_factor, blank,
+    doc_grad, pool_grad, held, units, upstream, inner, high, low, query_sem, unit_sem, row_sem,
 ):
-    step = pl.program_id(0)
-    block = queries.shape[1]
-    slots = unit.shape[0]
+    slots, width = unit.shape
     own = doc_unit.shape[0]
-    blank_rows = blank.shape[0]
-    fills = [
-        pltpu.make_async_copy(blank, pool_grad.at[pl.ds(i * blank_rows, blank_rows)], fill_sem.at[i])
-        for i in range(pool_grad.shape[0] // blank_rows)
-    ]
-
-    @pl.when(step == 0)
-    def _():
-        blank[...] = jnp.zeros_like(blank)
-        for fill in fills:
-            fill.start()
-        first, second = halves(weight[...])
-        high[...] = first
-        low[...] = second
-
-    right = halves(queries[...])
-    column = pl.multiple_of(step * block, block)
-    upstream[:, pl.ds(column, block)] = dot3((high[...], low[...]), right, ((1,), (0,)))
-
-    @pl.when(step == pl.num_programs(0) - 1)
-    def _():
-        for fill in fills:
-            fill.wait()
-        above = upstream[pl.ds(slots, own), :]
-        inner = jnp.sum(doc_unit[...] * above, axis=1, keepdims=True)
-        doc_grad[...] = doc_factor[:, :1] * (above - doc_unit[...] * inner)
-
-        def row_copy(j):
-            return pltpu.make_async_copy(
-                upstream.at[pl.ds(j, 1)], pool_grad.at[pl.ds(target[j], 1)], row_sem
-            )
-
-        def settle(tile, carry):
-            rows = pl.ds(pl.multiple_of(tile * 8, 8), 8)
-            above = upstream[rows, :]
-            unit_rows = unit[rows, :]
-            inner = jnp.sum(unit_rows * above, axis=1, keepdims=True)
-            upstream[rows, :] = factor[rows, :1] * (above - unit_rows * inner)
-            for i in range(8):
-                @pl.when(target[tile * 8 + i] >= 0)
-                def _():
-                    row_copy(tile * 8 + i).start()
-            return carry
-
-        lax.fori_loop(0, slots // 8, settle, 0)
-
-        def drain(j, carry):
-            @pl.when(target[j] >= 0)
-            def _():
-                row_copy(j).wait()
-            return carry
-
-        lax.fori_loop(0, slots, drain, 0)
-
-
-def finish(target, weight, queries, unit, factor, doc_unit, doc_factor, pool_rows):
+
+    def columns(i):
+        return pl.ds(pl.multiple_of(i * block, block), block)
+
+    def query_copy(i):
+        return pltpu.make_async_copy(
+            queries.at[:, columns(i)], held.at[:, columns(i)], query_sem.at[i]
+        )
+
+    def unit_copy(i):
+        return pltpu.make_async_copy(unit.at[:, columns(i)], units.at[:, columns(i)], unit_sem.at[i])
+
+    for i in range(width // block):
+        query_copy(i).start()
+        unit_copy(i).start()
+    inner[...] = jnp.zeros_like(inner)
+    first, second = halves(weight[...])
+    high[...] = first
+    low[...] = second
+
+    def multiply(i, carry):
+        query_copy(i).wait()
+        unit_copy(i).wait()
+        above = dot3((high[...], low[...]), halves(held[:, columns(i)]), ((1,), (0,)))
+        upstream[:, columns(i)] = above
+        product = above[:slots] * units[:, columns(i)]
+        part = product[:, :lanes]
+        for strip in range(1, block // lanes):
+            part = part + product[:, strip * lanes : (strip + 1) * lanes]
+        inner[...] += part
+        return carry
+
+    lax.fori_loop(0, width // block, multiply, 0)
+
+    above = upstream[pl.ds(slots, own), :]
+    along = jnp.sum(doc_unit[...] * above, axis=1, keepdims=True)
+    doc_grad[...] = doc_factor[:, :1] * (above - doc_unit[...] * along)
+
+    def settle(tile, carry):
+        rows = pl.ds(pl.multiple_of(tile * 16, 16), 16)
+        along = jnp.sum(inner[rows, :], axis=1, keepdims=True)
+        upstream[rows, :] = factor[rows, :1] * (upstream[rows, :] - units[rows, :] * along)
+        return carry
+
+    lax.fori_loop(0, slots // 16, settle, 0)
+
+    def row_copy(j):
+        return pltpu.make_async_copy(
+            upstream.at[pl.ds(slot_of[j], 1)], pool_grad.at[pl.ds(row_of[j], 1)], row_sem
+        )
+
+    def send(j, carry):
+        row_copy(j).start()
+        return carry
+
+    def drain(j, carry):
+        row_copy(j).wait()
+        return carry
+
+    lax.fori_loop(0, count[0], send, 0)
+    lax.fori_loop(0, count[0], drain, 0)
+
+
+def finish(count, slot_of, row_of, weight, queries, unit, factor, doc_unit, doc_factor, blank):
     slots, width = unit.shape
     own = doc_unit.shape[0]
     batch = queries.shape[0]
     block = 512
-    whole = lambda a: pl.BlockSpec(a.shape, lambda i, *_: (0, 0))
-    blank_rows = 64
+    total = slots + 2 * own
+    weight = jnp.pad(weight, ((0, total - weight.shape[0]), (0, 0)))
+    vmem = pl.BlockSpec(memory_space=pltpu.VMEM)
+    anywhere = pl.BlockSpec(memory_space=pl.ANY)
+    smem = pl.BlockSpec(memory_space=pltpu.SMEM)
     return pl.pallas_call(
-        finish_kernel,
-        grid_spec=pltpu.PrefetchScalarGridSpec(
-            num_scalar_prefetch=1,
-            grid=(width // block,),
-            in_specs=[
-                whole(weight),
-                pl.BlockSpec((batch, block), lambda i, *_: (0, i)),
-                whole(unit),
-                whole(factor),
-                whole(doc_unit),
-                whole(doc_factor),
-            ],
-            out_specs=[whole(doc_unit), pl.BlockSpec(memory_space=pl.ANY)],
-            scratch_shapes=[
-                pltpu.VMEM((slots + own, width), jnp.float32),
-                pltpu.VMEM((slots + own, batch), jnp.bfloat16),
-                pltpu.VMEM((slots + own, batch), jnp.bfloat16),
-                pltpu.VMEM((blank_rows, width), jnp.float32),
-                pltpu.SemaphoreType.DMA((pool_rows // blank_rows,)),
-                pltpu.SemaphoreType.DMA,
-            ],
-        ),
+        functools.partial(finish_kernel, block),
+        in_specs=[smem, smem, smem, vmem, anywhere, anywhere, vmem, vmem, vmem, anywhere],
+        out_specs=[vmem, anywhere],
+        scratch_shapes=[
+            pltpu.VMEM((batch, width), jnp.float32),
+            pltpu.VMEM((slots, width), jnp.float32),
+            pltpu.VMEM((total, width), jnp.float32),
+            pltpu.VMEM((slots, lanes), jnp.float32),
+            pltpu.VMEM((total, batch), jnp.bfloat16),
+            pltpu.VMEM((total, batch), jnp.bfloat16),
+            pltpu.SemaphoreType.DMA((width // block,)),
+            pltpu.SemaphoreType.DMA((width // block,)),
+            pltpu.SemaphoreType.DMA,
+        ],
         out_shape=[
             jax.ShapeDtypeStruct((own, width), jnp.float32),
-            jax.ShapeDtypeStruct((pool_rows, width), jnp.float32),
-        ],
+            jax.ShapeDtypeStruct(blank.shape, jnp.float32),
+        ],
+        input_output_aliases={9: 1},
         compiler_params=pltpu.CompilerParams(vmem_limit_bytes=limit),
         cost_estimate=pl.CostEstimate(
-            flops=6 * (slots + own) * batch * width, bytes_accessed=4 * width * (batch + pool_rows + slots), transcendentals=0
+            flops=6 * total * batch * width, bytes_accessed=4 * width * (batch + 2 * slots), transcendentals=0
         ),
-    )(target, weight, queries, unit, factor, doc_unit, doc_factor)
+    )(count, slot_of, row_of, weight, queries, unit, factor, doc_unit, doc_factor, blank)
 
 
 def factor_of(values):
@@ -269,7 +291,9 @@
     taken = slot[None, :] == jnp.arange(slots, dtype=jnp.int32)[:, None]
     request = jnp.sum(jnp.where(taken, code[None, :] + 1, 0), axis=1) - 1
     slot_query = jnp.sum(jnp.where(taken, asker[None, :] + 1, 0), axis=1) - 1
-    arrived = exchange(request.reshape(devices, capacity)).reshape(-1)
+    request = request.reshape(devices, capacity)
+    request = jnp.pad(request, ((0, 0), (0, lanes - capacity)), constant_values=-1)
+    arrived = exchange(request)[:, :capacity].reshape(-1)
 
     query_factor = factor_of(queries)
     doc_factor = factor_of(documents)
@@ -300,8 +324,9 @@
     for steps in range(1, pool_size):
         shares = shares + forward(payload[steps * own : (steps + 1) * own], steps)
 
-    neg_parts, neg_mixed = against(
-        neg_rows.reshape(slots * strips, lanes), query_unit, slot_query[None, :]
+    shares, slot_query = lax.optimization_barrier((shares, slot_query))
+    neg_parts, neg_mixed, blank = against(
+        neg_rows.reshape(slots * strips, lanes), query_unit, slot_query[None, :], pool_rows
     )
     totals = shares[:, width] + jnp.sum(neg_parts, axis=1)
     upstream = heat * ((shares[:, :width] + neg_mixed) / totals[:, None] - doc_unit)
@@ -343,16 +368,22 @@
     spread = dot(same.astype(jnp.float32), spread, ((1,), (0,)))
     slot_order = jnp.arange(slots, dtype=jnp.int32)
     repeated = jnp.any(same & (slot_order[None, :] < slot_order[:, None]), axis=1)
-    target = jnp.where(valid & ~repeated, named_row, -1)
+    written = valid & ~repeated
+    rank = jnp.cumsum(written.astype(jnp.int32)) - 1
+    listed = (rank[None, :] == slot_order[:, None]) & written[None, :]
+    slot_of = jnp.sum(jnp.where(listed, slot_order[None, :], 0), axis=1)
+    row_of = jnp.sum(jnp.where(listed, named_row[None, :], 0), axis=1)
     document_grad, pool_grad = finish(
-        target,
+        jnp.sum(written.astype(jnp.int32))[None],
+        slot_of,
+        row_of,
         jnp.concatenate([spread, doc_weight], axis=0),
         everything,
         row_unit,
         row_factor,
         doc_unit,
         jnp.broadcast_to(doc_factor, (own, lanes)),
-        pool_rows,
+        blank,
     )
     return (objective, query_grad, document_grad, pool_grad)
 

time: 213 us -> 198 us (0.930)
  waiting for transfers between devices: 88.5 us -> 74.6 us
  Pallas kernels: 45.4 us -> 39.2 us
  starting transfers between devices: 31 us -> 35.5 us
  other arithmetic: 12 us -> 14.2 us
    all_to_all x3, waiting for transfers between devices: 76.8 us -> 30.6 us  [exchange(): lax.all_to_all(values, everyone, split_axis=0, concat_axis=0, tiled=True)]
    ppermute x6, waiting for transfers between devices: 11.6 us -> 35.4 us  [forward(): lax.ppermute(values, 'pool', [(i, (i + steps) % pool_size) for i in range...]
    all_gather x1, waiting for transfers between devices: 0.01 us -> 8.6 us  [local(): everything = lax.all_gather(cohort, 'dp', axis=0, tiled=True)]
    pallas_call x1, Pallas kernels: 13.3 us -> 9.64 us  [pick(): pl.pallas_call(functools.partial(pick_kernel, step_rows), grid_spec=pltpu...]
    all_to_all x3, starting transfers between devices: 25.1 us -> 27.9 us  [exchange(): lax.all_to_all(values, everyone, split_axis=0, concat_axis=0, tiled=True)]
    pallas_call x2, Pallas kernels: 32.1 us -> 29.6 us  [the longest x1 17.7 us: finish(): pl.pallas_call(functools.partial(finish_kernel, block), in_specs=[smem, s...]
  transfers between devices with their start and end apart: 11 -> 11, of which waited for: 7 -> 7; matrix products, arithmetic and copies ran while one was open for 12% -> 14% of each run, Pallas kernels for 10% -> 11%
where the time goes in v1:
time: 198 us
  waiting for transfers between devices  74.6 us (38%)
  Pallas kernels  39.2 us (20%)
  starting transfers between devices  35.5 us (18%)
  between operations  16.3 us (8%)
  other arithmetic  14.2 us (7%)
  matrix products  11.6 us (6%)
  local copies, waits for them, and re-layouts  6.16 us (3%)
    ppermute x6, waiting for transfers between devices, forward(): lax.ppermute(values, 'pool', [(i, (i + steps) % pool_size) for i in range...  35.4 us
    all_to_all x3, waiting for transfers between devices, exchange(): lax.all_to_all(values, everyone, split_axis=0, concat_axis=0, tiled=True)  30.6 us
    all_to_all x3, starting transfers between devices, exchange(): lax.all_to_all(values, everyone, split_axis=0, concat_axis=0, tiled=True)  27.9 us
    pallas_call x1, Pallas kernels, finish(): pl.pallas_call(functools.partial(finish_kernel, block), in_specs=[smem, s...  17.7 us
    pallas_call x1, Pallas kernels, against(): pl.pallas_call(against_kernel, out_specs=[vmem, vmem, pl.BlockSpec(memory...  11.9 us
    dot_general x3, matrix products, dot(): lax.dot_general(left, right, (contract, ((), ())), precision=highest, pre...  11.6 us
    pallas_call x1, Pallas kernels, pick(): pl.pallas_call(functools.partial(pick_kernel, step_rows), grid_spec=pltpu...  9.64 us
    all_gather x1, waiting for transfers between devices, local(): everything = lax.all_gather(cohort, 'dp', axis=0, tiled=True)  8.6 us
  transfers between devices with their start and end apart: 11, of which 7 were waited for; matrix products, arithmetic and copies ran while one was open for 14% of the time, Pallas kernels for 11%

profile of v1, /device:TPU:1, one launch (start us, length us, event | category | flops | bytes accessed | tf_op | source)
XLA Modules:
  0.0 197.6 jit_solution(15672300301834842187)
XLA Ops:
  7.2 1.1 multiply_reduce_fusion.2
  8.3 1.6 broadcast_multiply_fusion.doc_unit
  11.9 11.5 %all-to-all-start = ((s32[128,1,128]{2,1,0:T(1,128)}), s32[128,1,128]{2,1,0:T(1,128)S(1)}, u32[]{:S(2)}, u32[]{:S(2)}) async-start(s32[128,1,128]{2,1,0:T(1,128)} %bitcast.1), calls=%async_computation | async-start | bytes 131072 | tf_op jit(solution)/shard_map/all_to_all | solution.py:282
  23.4 1.1 multiply_reduce_fusion.3
  25.5 7.5 %all-to-all-done = s32[128,1,128]{2,1,0:T(1,128)S(1)} async-done(((s32[128,1,128]{2,1,0:T(1,128)}), s32[128,1,128]{2,1,0:T(1,128)S(1)}, u32[]{:S(2)}, u32[]{:S(2)}) %all-to-all-start) | async-done | bytes 65568 | tf_op jit(solution)/shard_map/all_to_all | solution.py:282
  33.5 1.9 collective-permute-start.1
  36.2 5.2 %collective-permute-done = f32[8,4096]{1,0:T(8,128)S(1)} collective-permute-done((f32[8,4096]{1,0:T(8,128)S(1)}, f32[8,4096]{1,0:T(8,128)S(1)}, u32[]{:S(2)}, u32[]{:S(2)}) %collective-permute-start) | collective-permute-done | bytes 131104 | tf_op jit(solution)/shard_map/ppermute | solution.py:277
  42.9 9.6 %shard_map.75 = (f32[256,4096]{1,0:T(8,128)}, f32[256,128]{1,0:T(8,128)}, f32[8192,128]{1,0:T(8,128)}) custom-call(s32[256]{0:T(256)} %get-tuple-element.47.wanted, f32[512,4096]{1,0:T(8,128)} %pool.1), custom_call_target="tpu_custom_call" | custom-call | flops 4194304 | bytes 12582912 | tf_op jit(solution)/shard_map/pallas_call | solution.py:68
  52.6 12.2 %all-to-all-start.1 = ((f32[128,64,128]{2,1,0:T(8,128)}), f32[128,64,128]{2,1,0:T(8,128)}, u32[]{:S(2)}, u32[]{:S(2)}) async-start(f32[128,64,128]{2,1,0:T(8,128)} %bitcast.26), calls=%async_computation.1 | async-start | bytes 8388608 | tf_op jit(solution)/shard_map/all_to_all | solution.py:282
  67.8 6.0 %fusion.27 = (f32[32]{0:T(128)S(1)}, f32[32,256]{1,0:T(8,128)S(1)}) fusion(f32[32,4096]{1,0:T(8,128)S(1)} %copy-done.3, f32[256,4096]{1,0:T(8,128)} %all-gather.3.cloned.1.call-done), kind=kOutput, calls=%fused_computation.109 | convolution fusion | flops 402677728 | bytes 4751488 | tf_op jit(solution)/shard_map/dot_general | solution.py:253
  74.1 4.7 %fusion.28 = f32[32,4096]{1,0:T(8,128)S(1)} fusion(f32[32,256]{1,0:T(8,128)S(1)} %get-tuple-element.49, f32[256,4096]{1,0:T(8,128)} %all-gather.3.cloned.1.call-done), kind=kOutput, calls=%fused_computation.110 | convolution fusion | flops 402653184 | bytes 4751360 | tf_op jit(solution)/shard_map/dot_general | solution.py:253
  78.9 1.5 collective-permute-start.3
  80.4 1.3 collective-permute-start.5
  81.7 1.6 collective-permute-start.4
  83.4 24.9 %collective-permute-done.3 = f32[8,4224]{1,0:T(8,128)S(1)} collective-permute-done((f32[8,4224]{1,0:T(8,128)S(1)}, f32[8,4224]{1,0:T(8,128)S(1)}, u32[]{:S(2)}, u32[]{:S(2)}) %collective-permute-start.3) | collective-permute-done | bytes 135200 | tf_op jit(solution)/shard_map/ppermute | solution.py:277
  108.3 5.4 %collective-permute-done.4 = f32[8,4224]{1,0:T(8,128)S(1)} collective-permute-done((f32[8,4224]{1,0:T(8,128)S(1)}, f32[8,4224]{1,0:T(8,128)S(1)}, u32[]{:S(2)}, u32[]{:S(2)}) %collective-permute-start.4) | collective-permute-done | bytes 135200 | tf_op jit(solution)/shard_map/ppermute | solution.py:277
  113.7 12.3 %all-to-all-done.1 = f32[128,64,128]{2,1,0:T(8,128)} async-done(((f32[128,64,128]{2,1,0:T(8,128)}), f32[128,64,128]{2,1,0:T(8,128)}, u32[]{:S(2)}, u32[]{:S(2)}) %all-to-all-start.1) | async-done | bytes 4194336 | tf_op jit(solution)/shard_map/all_to_all | solution.py:282
  126.0 11.9 %shard_map.76 = (f32[8,256]{1,0:T(8,128)}, f32[8,4096]{1,0:T(8,128)}, f32[512,4096]{1,0:T(8,128)}) custom-call(f32[8192,128]{1,0:T(8,128)} %bitcast.6.packed, f32[8,4096]{1,0:T(8,128)} %copy-done, s32[1,256]{1,0:T(1,128)} %bitcast.34), custom_call_target="tpu_custom_call" | custom-call | flops 100663296 | bytes 12582912 | tf_op jit(solution)/shard_map/pallas_call | solution.py:122
  139.0 1.2 multiply_reduce_fusion
  142.2 4.3 %all-to-all-start.2 = ((f32[128,1,274]{2,1,0:T(1,128)}), f32[128,1,274]{2,1,0:T(1,128)S(1)}, u32[]{:S(2)}, u32[]{:S(2)}) async-start(f32[128,1,274]{2,1,0:T(1,128)} %copy.49), calls=%async_computation.2 | async-start | bytes 393216 | tf_op jit(solution)/shard_map/all_to_all | solution.py:282
  147.2 10.8 %all-to-all-done.2 = f32[128,1,274]{2,1,0:T(1,128)S(1)} async-done(((f32[128,1,274]{2,1,0:T(1,128)}), f32[128,1,274]{2,1,0:T(1,128)S(1)}, u32[]{:S(2)}, u32[]{:S(2)}) %all-to-all-start.2) | async-done | bytes 140320 | tf_op jit(solution)/shard_map/all_to_all | solution.py:282
  161.5 1.1 select_maximum_fusion.weight
  162.7 8.6 %all-gather.5.cloned.1.call-done.queries = f32[1024,4096]{1,0:T(8,128)} async-done(((f32[32,4096]{1,0:T(8,128)}), f32[1024,4096]{1,0:T(8,128)}) %all-gather.5.cloned.1.call-update) | async-done | bytes 16777232 | tf_op jit(solution)/shard_map/all_gather | solution.py:317
  171.9 17.7 %shard_map.77 = (f32[8,4096]{1,0:T(8,128)}, f32[512,4096]{1,0:T(8,128)}) custom-call(s32[1]{0:T(128)} %bitcast.11.count, s32[256]{0:T(256)} %get-tuple-element.33.slot_of, s32[256]{0:T(256)} %get-tuple-element.32.row_of, f32[272,1024]{1,0:T(8,128)} %select_maximum_fusion.weight, ...), custom_call_target="tpu_custom_call", output_to_operand_aliasing={{1}: (9, {})} | custom-call | flops 6845104128 | bytes 25165824 | tf_op jit(solution)/shard_map/pallas_call | solution.py:221
  (95 shorter events, 16.5 us)
Async XLA Ops:
  7.2 60.6 %all-gather.3.cloned.1.call-start = ((), (), s32[]{:S(2)}) async-start(), calls=%async_computation.3 | async-start | bytes 4325376 | tf_op jit(solution)/shard_map/all_gather | solution.py:316
  11.9 21.1 %all-to-all-start = ((s32[128,1,128]{2,1,0:T(1,128)}), s32[128,1,128]{2,1,0:T(1,128)S(1)}, u32[]{:S(2)}, u32[]{:S(2)}) async-start(s32[128,1,128]{2,1,0:T(1,128)} %bitcast.1), calls=%async_computation | async-start | bytes 131072 | tf_op jit(solution)/shard_map/all_to_all | solution.py:282
  23.4 147.9 %all-gather.5.cloned.1.call-start = ((), (), s32[]{:S(2)}) async-start(), calls=%async_computation.4 | async-start | bytes 17301504 | tf_op jit(solution)/shard_map/all_gather | solution.py:317
  25.5 27.1 %copy-start = (f32[8,4096]{1,0:T(8,128)}, f32[8,4096]{1,0:T(8,128)S(1)}, u32[]{:S(2)}) copy-start(f32[8,4096]{1,0:T(8,128)S(1)} %broadcast_multiply_fusion.1.unit) | copy-start | bytes 393220
  33.1 8.4 %collective-permute-start.2 = (f32[8,4096]{1,0:T(8,128)S(1)}, f32[8,4096]{1,0:T(8,128)S(1)}, u32[]{:S(2)}, u32[]{:S(2)}) collective-permute-start(f32[8,4096]{1,0:T(8,128)S(1)} %broadcast_multiply_fusion.1.unit), channel_id=1, source_target_pairs={{0,1},{1,2},{2,3},{3,0},{4,5},{5,6},{6,7},{7,4},{8,9},{9,10},{10,1... | collective-permute-start | bytes 393224 | tf_op jit(solution)/shard_map/ppermute | solution.py:277
  33.5 7.9 %collective-permute-start.1 = (f32[8,4096]{1,0:T(8,128)S(1)}, f32[8,4096]{1,0:T(8,128)S(1)}, u32[]{:S(2)}, u32[]{:S(2)}) collective-permute-start(f32[8,4096]{1,0:T(8,128)S(1)} %broadcast_multiply_fusion.1.unit), channel_id=1, source_target_pairs={{0,2},{1,3},{2,0},{3,1},{4,6},{5,7},{6,4},{7,5},{8,10},{9,11},{10,... | collective-permute-start | bytes 393224 | tf_op jit(solution)/shard_map/ppermute | solution.py:277
  35.4 6.0 %collective-permute-start = (f32[8,4096]{1,0:T(8,128)S(1)}, f32[8,4096]{1,0:T(8,128)S(1)}, u32[]{:S(2)}, u32[]{:S(2)}) collective-permute-start(f32[8,4096]{1,0:T(8,128)S(1)} %broadcast_multiply_fusion.1.unit), channel_id=1, source_target_pairs={{0,3},{1,0},{2,1},{3,2},{4,7},{5,4},{6,5},{7,6},{8,11},{9,8},{10,9... | collective-permute-start | bytes 393224 | tf_op jit(solution)/shard_map/ppermute | solution.py:277
  41.5 0.8 copy-start.2
  52.5 13.0 %copy-start.5 = (s32[256]{0:T(256)S(1)}, s32[256]{0:T(256)}, u32[]{:S(2)}) copy-start(s32[256]{0:T(256)} %get-tuple-element.47.wanted) | copy-start | bytes 3076
  52.5 15.2 %copy-start.3 = (f32[32,4096]{1,0:T(8,128)S(1)}, f32[32,4096]{1,0:T(8,128)}, u32[]{:S(2)}) copy-start(f32[32,4096]{1,0:T(8,128)} %copy-done.2) | copy-start | bytes 1572868
  52.6 73.4 %all-to-all-start.1 = ((f32[128,64,128]{2,1,0:T(8,128)}), f32[128,64,128]{2,1,0:T(8,128)}, u32[]{:S(2)}, u32[]{:S(2)}) async-start(f32[128,64,128]{2,1,0:T(8,128)} %bitcast.26), calls=%async_computation.1 | async-start | bytes 8388608 | tf_op jit(solution)/shard_map/all_to_all | solution.py:282
  78.8 60.1 %copy-start.1 = (f32[8,4096]{1,0:T(8,128)S(1)}, f32[8,4096]{1,0:T(8,128)}, u32[]{:S(2)}) copy-start(f32[8,4096]{1,0:T(8,128)} %copy-done) | copy-start | bytes 393220
  78.8 60.1 %copy-start.4 = (f32[8,4096]{1,0:T(8,128)S(1)}, f32[8,4096]{1,0:T(8,128)}, u32[]{:S(2)}) copy-start(f32[8,4096]{1,0:T(8,128)} %param.5) | copy-start | bytes 393220
  78.9 29.4 %collective-permute-start.3 = (f32[8,4224]{1,0:T(8,128)S(1)}, f32[8,4224]{1,0:T(8,128)S(1)}, u32[]{:S(2)}, u32[]{:S(2)}) collective-permute-start(f32[8,4224]{1,0:T(8,128)S(1)} %get-tuple-element.41), channel_id=1, source_target_pairs={{0,1},{1,2},{2,3},{3,0},{4,5},{5,6},{6,7},{7,4},{8,9},{9,10},{10,1... | collective-permute-start | bytes 405512 | tf_op jit(solution)/shard_map/ppermute | solution.py:277
  80.4 27.9 %collective-permute-start.5 = (f32[8,4224]{1,0:T(8,128)S(1)}, f32[8,4224]{1,0:T(8,128)S(1)}, u32[]{:S(2)}, u32[]{:S(2)}) collective-permute-start(f32[8,4224]{1,0:T(8,128)S(1)} %get-tuple-element.42), channel_id=1, source_target_pairs={{0,3},{1,0},{2,1},{3,2},{4,7},{5,4},{6,5},{7,6},{8,11},{9,8},{10,9... | collective-permute-start | bytes 405512 | tf_op jit(solution)/shard_map/ppermute | solution.py:277
  81.7 31.9 %collective-permute-start.4 = (f32[8,4224]{1,0:T(8,128)S(1)}, f32[8,4224]{1,0:T(8,128)S(1)}, u32[]{:S(2)}, u32[]{:S(2)}) collective-permute-start(f32[8,4224]{1,0:T(8,128)S(1)} %get-tuple-element.43), channel_id=1, source_target_pairs={{0,2},{1,3},{2,0},{3,1},{4,6},{5,7},{6,4},{7,5},{8,10},{9,11},{10,... | collective-permute-start | bytes 405512 | tf_op jit(solution)/shard_map/ppermute | solution.py:277
  142.2 15.8 %all-to-all-start.2 = ((f32[128,1,274]{2,1,0:T(1,128)}), f32[128,1,274]{2,1,0:T(1,128)S(1)}, u32[]{:S(2)}, u32[]{:S(2)}) async-start(f32[128,1,274]{2,1,0:T(1,128)} %copy.49), calls=%async_computation.2 | async-start | bytes 393216 | tf_op jit(solution)/shard_map/all_to_all | solution.py:282
Sparse Core Ops, SparseCore 0:
  10.3 50.2 all-gather.2
  62.9 108.3 all-gather.4
